TPU v7x, 256 devices: a whole 4x4x8 slice. The times are simulated.
256 devices in a mesh: ctx: 32 (over y, z), head: 8 (over x, core).
Axes of the slice: x: 4, y: 4, z: 8, core: 2. Of those that a mesh axis runs over, the one named last changes fastest.
Arguments:
- lin_query: bfloat16 [65536, 3072], P('ctx', 'head'), may hold values from -6 to 6
- lin_key: bfloat16 [65536, 3072], P('ctx', 'head'), may hold values from -6 to 6
- lin_value: bfloat16 [65536, 3072], P('ctx', 'head'), may hold values from -6 to 6
- log_decay: float32 [24, 65536], P('head', 'ctx'), may hold values from -1 to 0, as said below
- norm_gain: float32 [3072], P('head'), may hold values from 0.25 to 1.75
- soft_query: bfloat16 [65536, 3072], P(('ctx', 'head')), may hold values from -12 to 12
- soft_key: bfloat16 [65536, 3072], P(('ctx', 'head')), may hold values from -12 to 12
- block_list: int32 [512, 16], P('ctx'), may hold values from -1 to 511, as said below
Outputs:
- lin_out: bfloat16 [65536, 3072], P('ctx', 'head')
- soft_out: bfloat16 [65536, 3072], P(('ctx', 'head'))
Inputs may be any that keep to these rules, and one draw needn't show every extreme that they name: `block_list`: entry j of query block b is a key block from b - 32 to b, or -1 where that block would lie before the first; entry 0 is b itself, entry 1 is b - 32 (or -1); entries may repeat. `log_decay`: negative log decays.
All inputs are finite; a program needn't handle non-finite values.
Results may differ from a plain program's by a relative error of at most 0.0051.
Values may be sent and summed in bfloat16 or wider, within the bound.
A program may use at most 128 MiB of HBM per device.

v0:
```python
import jax
import jax.numpy as jnp
from jax import lax
from jax.sharding import PartitionSpec as P

HD = 128
BLK = 128
NB = 16


HIGHEST = lax.Precision.HIGHEST
EPSILON = 1e-06


def carried_in(array, axis, combine, identity):
    size, index = (lax.axis_size(axis), lax.axis_index(axis))
    everything = jax.tree.map(lambda part: lax.all_gather(part, axis), array)
    start = jax.tree.map(
        lambda part, zero: jnp.broadcast_to(jnp.asarray(zero, part.dtype), part.shape),
        array,
        identity,
    )

    def turn(k, before):
        reached = k < index
        new = combine(before, jax.tree.map(lambda part: part[k], everything))
        return jax.tree.map(lambda a, b: jnp.where(reached, a, b), new, before)

    return lax.fori_loop(0, size, turn, start)


def passed_along(array, axis, by):
    size = lax.axis_size(axis)
    pairs = [(i, i + by) for i in range(size) if 0 <= i + by < size]
    return lax.ppermute(array, axis, pairs)


def silu_round(inputs):
    values = inputs.astype(jnp.float32)
    return (values / (1.0 + jnp.exp(-values))).astype(jnp.bfloat16)


def link_states(earlier, later):
    return (earlier[0] * later[0], later[0][:, None, None] * earlier[1] + later[1])


def lightning(lin_query, lin_key, lin_value, log_decay, norm_gain):
    tokens, local_width = lin_query.shape
    head_count = log_decay.shape[0]
    blocks = tokens // BLK

    def to_blocks(array):
        return array.reshape(blocks, BLK, head_count, HD).transpose(2, 0, 1, 3)

    feat_query = to_blocks(silu_round(lin_query))
    feat_key = to_blocks(silu_round(lin_key))
    values = to_blocks(lin_value)
    cumulated = jnp.cumsum(log_decay.reshape(head_count, blocks, BLK), axis=2)
    block_total = cumulated[:, :, -1]
    causal = jnp.arange(BLK)[:, None] >= jnp.arange(BLK)[None, :]
    raw_scores = jnp.einsum(
        "hnte,hnse->hnts", feat_query, feat_key, preferred_element_type=jnp.float32
    )
    decay_gap = jnp.where(causal, cumulated[:, :, :, None] - cumulated[:, :, None, :], -1e30)
    intra_weights = (raw_scores * jnp.exp(decay_gap)).astype(jnp.bfloat16)
    intra_part = jnp.einsum(
        "hnts,hnse->hnte", intra_weights, values, preferred_element_type=jnp.float32
    )
    value_f = values.astype(jnp.float32)
    weighted = (
        feat_key.astype(jnp.float32) * jnp.exp(block_total[:, :, None] - cumulated)[:, :, :, None]
    )
    update = jnp.einsum("hnse,hnsf->hnef", weighted, value_f, precision=HIGHEST)

    def advance(kv_state, inputs):
        step_total, step_update = inputs
        return (jnp.exp(step_total)[:, None, None] * kv_state + step_update, kv_state)

    empty_state = jnp.zeros((head_count, HD, HD), jnp.float32)
    local_end, local_before = lax.scan(
        advance, empty_state, (block_total.T, update.transpose(1, 0, 2, 3))
    )
    shard_decay = jnp.exp(jnp.sum(block_total, axis=1))
    identity = (jnp.ones_like(shard_decay), jnp.zeros_like(local_end))
    incoming = carried_in((shard_decay, local_end), "ctx", link_states, identity)[1]
    lead_decay = jnp.cumsum(block_total, axis=1) - block_total
    states = (
        local_before.transpose(1, 0, 2, 3)
        + jnp.exp(lead_decay)[:, :, None, None] * incoming[:, None]
    )
    scaled_query = feat_query.astype(jnp.float32) * jnp.exp(cumulated)[:, :, :, None]
    inter_part = jnp.einsum("hnte,hnef->hntf", scaled_query, states, precision=HIGHEST)
    mixed = intra_part + inter_part
    mean_square = jnp.mean(mixed * mixed, axis=-1, keepdims=True)
    gain_rows = norm_gain.reshape(head_count, 1, 1, HD)
    normed = mixed * lax.rsqrt(mean_square + EPSILON) * gain_rows
    return normed.astype(jnp.bfloat16).transpose(1, 2, 0, 3).reshape(tokens, local_width)


def sparse_softmax(soft_query, soft_key, value_rows, block_list):
    queries, keys_mine = (
        lax.all_to_all(soft_query, "head", split_axis=1, concat_axis=0, tiled=True),
        lax.all_to_all(soft_key, "head", split_axis=1, concat_axis=0, tiled=True),
    )
    carried = (keys_mine, value_rows)
    fetched = []
    for relay_step in range(2):
        carried = passed_along((carried[0], carried[1]), "ctx", 1)
        fetched.insert(0, carried)
    tokens, local_width = queries.shape
    head_count = local_width // HD
    blocks = tokens // BLK
    near_keys = jnp.concatenate([fetched[0][0], fetched[1][0], keys_mine], axis=0).reshape(
        3 * blocks, BLK, local_width
    )
    near_values = jnp.concatenate([fetched[0][1], fetched[1][1], value_rows], axis=0).reshape(
        3 * blocks, BLK, local_width
    )
    position = lax.axis_index("ctx")
    first_block = (position - 2) * blocks
    own_ids = position * blocks + jnp.arange(blocks, dtype=jnp.int32)
    earlier = jnp.arange(NB)[:, None] > jnp.arange(NB)[None, :]
    repeat = jnp.any((block_list[:, :, None] == block_list[:, None, :]) & earlier[None], axis=2)
    usable = (block_list >= 0) & jnp.logical_not(repeat)
    local_index = jnp.where(block_list >= 0, block_list - first_block, 0)
    own_block = block_list == own_ids[:, None]
    group_size = min(4, blocks)
    group_count = blocks // group_size
    causal = jnp.arange(BLK)[:, None] >= jnp.arange(BLK)[None, :]
    scale = HD ** (-0.5)

    def attend(inputs):
        query_group, slot_index, slot_live, slot_own = inputs
        key_blocks = near_keys[slot_index].reshape(group_size, NB, BLK, head_count, HD)
        value_blocks = near_values[slot_index].reshape(group_size, NB, BLK, head_count, HD)
        logits = (
            jnp.einsum(
                "gthe,gjshe->ghtjs", query_group, key_blocks, preferred_element_type=jnp.float32
            )
            * scale
        )
        allowed = slot_live[:, None, None, :, None] & (
            jnp.logical_not(slot_own)[:, None, None, :, None] | causal[None, None, :, None, :]
        )
        masked = jnp.where(allowed, logits, -jnp.inf)
        row_max = jnp.max(masked, axis=(3, 4), keepdims=True)
        weights = jnp.exp(masked - row_max)
        row_total = jnp.sum(weights, axis=(3, 4))
        mixed = jnp.einsum(
            "ghtjs,gjshe->gthe",
            weights.astype(jnp.bfloat16),
            value_blocks,
            preferred_element_type=jnp.float32,
        )
        return (mixed / row_total.transpose(0, 2, 1)[:, :, :, None]).astype(jnp.bfloat16)

    grouped = (
        queries.reshape(group_count, group_size, BLK, head_count, HD),
        local_index.reshape(group_count, group_size, NB),
        usable.reshape(group_count, group_size, NB),
        own_block.reshape(group_count, group_size, NB),
    )
    outputs = lax.map(attend, grouped).reshape(tokens, local_width)
    return lax.all_to_all(outputs, "head", split_axis=0, concat_axis=1, tiled=True)


def shards(lin_query, lin_key, lin_value, log_decay, norm_gain, soft_query, soft_key, block_list):
    lin_out = lightning(lin_query, lin_key, lin_value, log_decay, norm_gain)
    soft_out = sparse_softmax(soft_query, soft_key, lin_out, block_list)
    return (lin_out, soft_out)


def solution(mesh):
    placed = (
        P("ctx", "head"),
        P("ctx", "head"),
        P("ctx", "head"),
        P("head", "ctx"),
        P("head"),
        P(("ctx", "head"), None),
        P(("ctx", "head"), None),
        P("ctx", None),
    )
    return jax.shard_map(
        shards,
        mesh=mesh,
        in_specs=placed,
        out_specs=(P("ctx", "head"), P(("ctx", "head"), None)),
        check_vma=False,
    )
```

profile of v0, /device:TPU:16, one launch (start us, length us, event | category | flops | bytes accessed | tf_op | source)
XLA Modules:
  0.0 641.1 jit_solution(14028825871638296190)
XLA Ops:
  9.1 2.3 fusion.44
  17.0 1.7 copy.135
  19.1 2.0 copy.138
  21.1 2.6 convert_multiply_fusion
  23.7 4.0 fusion.52
  27.7 27.9 %while.39 = (s32[]{:T(128)}, f32[3,128,128]{2,1,0:T(8,128)S(1)}, f32[16,3,128,128]{3,2,1,0:T(8,128)}, f32[16,3]{1,0:T(8,128)S(1)}, f32[16,3,128,128]{3,2,0,1:T(8,128)}, /*index=5*/s32[]{:T(128)}, s32[]{:T(128)}) while((s32[]{:T(128)}, f32[3,128,128]{2,1,0:T(8,128)S(1)}, f32[16,3,128,128]{3,2,1,0:T(8,128)}, f32[16,3]{1,0:T(8,128)S(1)}, ...), condition=%wide.region_2.3_spmd.clone, body=%wide.region_1.2_spmd.clone.sunk | while | flops 196611 | bytes 983184 | solution.py:80
  56.3 2.6 copy.147
  58.9 2.6 copy.148
  61.5 4.3 all-to-all-start.1
  67.3 66.3 %all-reduce = f32[96]{0:T(128)S(1)} all-reduce(f32[96]{0:T(128)S(1)} %exponential_dynamic-update-slice_fusion), channel_id=2, replica_groups=mesh['ctx'=32,'head'=8] {'ctx'}, use_global_device_ids=true, to_apply=%add | all-reduce | flops 96 | bytes 768
  133.9 2.1 collective-permute-start.2
  136.0 24.0 %all-gather.4.cloned.1.call-done = f32[96,128,128]{2,1,0:T(8,128)} async-done(((f32[3,128,128]{2,1,0:T(8,128)}), f32[96,128,128]{2,1,0:T(8,128)}) %all-gather.4.cloned.1.call-update) | async-done | bytes 6291472 | tf_op jit(solution)/shard_map/all_gather | solution.py:17
  159.9 34.1 %while.40 = (s32[]{:T(128)}, f32[3,128,128]{2,1,0:T(8,128)S(1)}, s32[]{:T(128)}, f32[32,3]{1,0:T(8,128)S(1)}, f32[32,3,128,128]{3,2,1,0:T(8,128)}, /*index=5*/s32[]{:T(128)}, s32[]{:T(128)}) while((s32[]{:T(128)}, f32[3,128,128]{2,1,0:T(8,128)S(1)}, s32[]{:T(128)}, f32[32,3]{1,0:T(8,128)S(1)}, f32[32,3,128,128]{3,2,1,0:T(8,128)}, ...), condition=%wide.region_6.7_spmd.clone, body=%wide.region_5.6_spmd.clone.sunk | while | flops 196612 | bytes 589973 | solution.py:29
  194.0 9.2 %fusion.47 = f32[3,16,128,128]{2,3,1,0:T(8,128)} fusion(f32[3,16,128,128]{2,1,3,0:T(8,128)S(1)} %get-tuple-element.358, f32[16,3,128,128]{3,2,1,0:T(8,128)} %get-tuple-element.171, f32[3,128,128]{2,1,0:T(8,128)S(1)} %get-tuple-element.173, f32[3,16]{0,1:T(8,128)S(1)} %copy.141), kind=kOutput, calls=%fused_computation.53 | convolution fusion | flops 1209532416 | bytes 9633984 | tf_op jit(solution)/shard_map/hnte,hnef->hntf/dot_general | solution.py:92
  203.2 5.6 multiply_reduce_fusion
  210.8 2.6 collective-permute-start
  213.4 3.2 collective-permute-start.3
  218.2 4.9 all-to-all-start
  223.1 30.0 %collective-permute-done = bf16[2048,384]{0,1:T(8,128)(2,1)} collective-permute-done((bf16[2048,384]{0,1:T(8,128)(2,1)S(1)}, bf16[2048,384]{0,1:T(8,128)(2,1)}, u32[]{:S(2)}, u32[]{:S(2)}) %collective-permute-start) | collective-permute-done | bytes 1572896 | tf_op jit(solution)/shard_map/ppermute | solution.py:35
  253.1 1.9 collective-permute-start.1
  255.6 2.0 copy.146
  257.6 3.5 reshape.179
  261.1 25.7 %collective-permute-done.3 = bf16[2048,384]{1,0:T(8,128)(2,1)} collective-permute-done((bf16[2048,384]{1,0:T(8,128)(2,1)}, bf16[2048,384]{1,0:T(8,128)(2,1)}, u32[]{:S(2)}, u32[]{:S(2)}) %collective-permute-start.3) | collective-permute-done | bytes 1572896 | tf_op jit(solution)/shard_map/ppermute | solution.py:35
  286.8 5.4 pad_maximum_fusion.1
  292.2 26.2 %collective-permute-done.1 = bf16[2048,384]{0,1:T(8,128)(2,1)} collective-permute-done((bf16[2048,384]{0,1:T(8,128)(2,1)}, bf16[2048,384]{0,1:T(8,128)(2,1)}, u32[]{:S(2)}, u32[]{:S(2)}) %collective-permute-start.1) | collective-permute-done | bytes 1572896 | tf_op jit(solution)/shard_map/ppermute | solution.py:35
  318.4 3.7 pad_maximum_fusion
  322.2 6.6 %copy.159 = bf16[6144,384]{1,0:T(8,128)(2,1)} copy(bf16[6144,384]{0,1:T(8,128)(2,1)} %pad_maximum_fusion) | data formatting | bytes 9437184
  328.8 273.7 %while.38 = (s32[]{:T(128)}, bf16[4,4,128,3,128]{2,1,0,4,3:T(4,128)(2,1)}, s32[4,4,16]{2,1,0:T(4,128)S(1)}, bf16[48,128,384]{2,1,0:T(8,128)(2,1)}, pred[4,4,16]{...) while((s32[]{:T(128)}, ...), condition=%wide.region_12.13_spmd.clone, body=%wide.region_9.12_spmd.clone.sunk | while | flops 1647720704 | bytes 175182128 | solution.py:163
  330.4 6.7 %gather_fusion = bf16[64,128,384]{2,1,0:T(8,128)(2,1)} fusion(bf16[48,128,384]{2,1,0:T(8,128)(2,1)} %get-tuple-element.545, s32[1024]{0:T(1024)S(1)} %pad_clamp_fusion.2), kind=kCustom, calls=%fused_computation.1.clone.clone.1 | custom fusion | bytes 12583168 | tf_op jit(solution)/shard_map/while/body/eval_jaxpr/gather | solution.py:134
  337.1 8.6 %copy.212 = bf16[64,128,384]{1,2,0:T(8,128)(2,1)} copy(bf16[64,128,384]{2,1,0:T(8,128)(2,1)} %gather_fusion) | data formatting | bytes 12582912 | tf_op jit(solution)/shard_map/while/body/eval_jaxpr/gather | solution.py:134
  345.7 8.6 %copy.213 = bf16[4,16,128,3,128]{4,2,1,3,0:T(8,128)(2,1)} copy(bf16[4,16,128,3,128]{2,4,3,1,0:T(8,128)(2,1)} %bitcast.171) | data formatting | bytes 12582912 | tf_op jit(solution)/shard_map/while/body/eval_jaxpr/reshape | solution.py:134
  355.8 9.4 %fusion.81 = (f32[4,3,128]{2,1,0:T(4,128)S(1)}, f32[4,3,128,2048]{2,3,1,0}) fusion(pred[4,128,16,128]{1,3,2,0:T(8,128)(4,1)S(1)} %or_and_fusion.2, bf16[4,3,128,2048]{2,3,1,0:T(8,128)(2,1)} %bitcast.172, bf16[1,4,128,3,128]{4,2,3,1,0:T(8,128)(2,1)S(1)} %copy.214), kind=kOutput, calls=%fused_computation.5.clone.1 | convolution fusion | flops 814742016 | bytes 20322304 | tf_op jit(solution)/shard_map/while
  365.2 6.4 gather_fusion.1
  371.5 8.6 %copy.215 = bf16[64,128,384]{1,2,0:T(8,128)(2,1)} copy(bf16[64,128,384]{2,1,0:T(8,128)(2,1)} %gather_fusion.1) | data formatting | bytes 12582912 | tf_op jit(solution)/shard_map/while/body/eval_jaxpr/gather | solution.py:135
  380.1 7.7 %fusion.82 = f32[4,3,128]{2,1,0:T(4,128)S(1)} fusion(f32[4,3,128,2048]{2,3,1,0} %get-tuple-element.466, f32[4,3,128]{2,1,0:T(4,128)S(1)} %get-tuple-element.467, pred[4,128,16,128]{1,3,2,0:T(8,128)(4,1)} %copy-done.1), kind=kLoop, calls=%fused_computation.6.clone.1 | loop fusion | flops 12581376 | bytes 13643776 | tf_op jit(solution)/shard_map/while/body/eval_jaxpr/reduce_sum | solution.py:148
  388.6 7.5 %fusion.83 = bf16[1,4,128,3,128]{2,4,3,1,0:T(8,128)(2,1)S(1)} fusion(f32[4,3,128,2048]{2,3,1,0:S(1)} %copy-done, f32[4,3,128]{2,1,0:T(4,128)S(1)} %get-tuple-element.467, pred[4,128,16,128]{1,3,2,0:T(8,128)(4,1)} %copy-done.1, bf16[4,16,128,3,128]{2,4,3,1,0:T(8,128)(2,1)} %bitcast.175, f32[4,128,3]{1,2,0:T(4,128)S(1)} %bitcast.192), kind=kOutput, calls=%fused_computation.18.clone.1 | convolution fusion | flops 818282496 | bytes 20328448 | tf_op jit(solution)/shard_map/while/body/eval_jaxpr/ghtjs,gjshe->gthe/dot_general | solution.py:149
  398.9 6.7 %gather_fusion = bf16[64,128,384]{2,1,0:T(8,128)(2,1)} fusion(bf16[48,128,384]{2,1,0:T(8,128)(2,1)} %get-tuple-element.545, s32[1024]{0:T(1024)S(1)} %pad_clamp_fusion.2), kind=kCustom, calls=%fused_computation.1.clone.clone.1 | custom fusion | bytes 12583168 | tf_op jit(solution)/shard_map/while/body/eval_jaxpr/gather | solution.py:134
  405.5 8.6 %copy.212 = bf16[64,128,384]{1,2,0:T(8,128)(2,1)} copy(bf16[64,128,384]{2,1,0:T(8,128)(2,1)} %gather_fusion) | data formatting | bytes 12582912 | tf_op jit(solution)/shard_map/while/body/eval_jaxpr/gather | solution.py:134
  414.1 8.6 %copy.213 = bf16[4,16,128,3,128]{4,2,1,3,0:T(8,128)(2,1)} copy(bf16[4,16,128,3,128]{2,4,3,1,0:T(8,128)(2,1)} %bitcast.171) | data formatting | bytes 12582912 | tf_op jit(solution)/shard_map/while/body/eval_jaxpr/reshape | solution.py:134
  424.2 9.4 %fusion.81 = (f32[4,3,128]{2,1,0:T(4,128)S(1)}, f32[4,3,128,2048]{2,3,1,0}) fusion(pred[4,128,16,128]{1,3,2,0:T(8,128)(4,1)S(1)} %or_and_fusion.2, bf16[4,3,128,2048]{2,3,1,0:T(8,128)(2,1)} %bitcast.172, bf16[1,4,128,3,128]{4,2,3,1,0:T(8,128)(2,1)S(1)} %copy.214), kind=kOutput, calls=%fused_computation.5.clone.1 | convolution fusion | flops 814742016 | bytes 20322304 | tf_op jit(solution)/shard_map/while
  433.6 6.4 gather_fusion.1
  440.0 8.6 %copy.215 = bf16[64,128,384]{1,2,0:T(8,128)(2,1)} copy(bf16[64,128,384]{2,1,0:T(8,128)(2,1)} %gather_fusion.1) | data formatting | bytes 12582912 | tf_op jit(solution)/shard_map/while/body/eval_jaxpr/gather | solution.py:135
  448.6 7.7 %fusion.82 = f32[4,3,128]{2,1,0:T(4,128)S(1)} fusion(f32[4,3,128,2048]{2,3,1,0} %get-tuple-element.466, f32[4,3,128]{2,1,0:T(4,128)S(1)} %get-tuple-element.467, pred[4,128,16,128]{1,3,2,0:T(8,128)(4,1)} %copy-done.1), kind=kLoop, calls=%fused_computation.6.clone.1 | loop fusion | flops 12581376 | bytes 13643776 | tf_op jit(solution)/shard_map/while/body/eval_jaxpr/reduce_sum | solution.py:148
  457.0 7.5 %fusion.83 = bf16[1,4,128,3,128]{2,4,3,1,0:T(8,128)(2,1)S(1)} fusion(f32[4,3,128,2048]{2,3,1,0:S(1)} %copy-done, f32[4,3,128]{2,1,0:T(4,128)S(1)} %get-tuple-element.467, pred[4,128,16,128]{1,3,2,0:T(8,128)(4,1)} %copy-done.1, bf16[4,16,128,3,128]{2,4,3,1,0:T(8,128)(2,1)} %bitcast.175, f32[4,128,3]{1,2,0:T(4,128)S(1)} %bitcast.192), kind=kOutput, calls=%fused_computation.18.clone.1 | convolution fusion | flops 818282496 | bytes 20328448 | tf_op jit(solution)/shard_map/while/body/eval_jaxpr/ghtjs,gjshe->gthe/dot_general | solution.py:149
  467.3 6.7 %gather_fusion = bf16[64,128,384]{2,1,0:T(8,128)(2,1)} fusion(bf16[48,128,384]{2,1,0:T(8,128)(2,1)} %get-tuple-element.545, s32[1024]{0:T(1024)S(1)} %pad_clamp_fusion.2), kind=kCustom, calls=%fused_computation.1.clone.clone.1 | custom fusion | bytes 12583168 | tf_op jit(solution)/shard_map/while/body/eval_jaxpr/gather | solution.py:134
  473.9 8.6 %copy.212 = bf16[64,128,384]{1,2,0:T(8,128)(2,1)} copy(bf16[64,128,384]{2,1,0:T(8,128)(2,1)} %gather_fusion) | data formatting | bytes 12582912 | tf_op jit(solution)/shard_map/while/body/eval_jaxpr/gather | solution.py:134
  482.5 8.6 %copy.213 = bf16[4,16,128,3,128]{4,2,1,3,0:T(8,128)(2,1)} copy(bf16[4,16,128,3,128]{2,4,3,1,0:T(8,128)(2,1)} %bitcast.171) | data formatting | bytes 12582912 | tf_op jit(solution)/shard_map/while/body/eval_jaxpr/reshape | solution.py:134
  492.6 9.4 %fusion.81 = (f32[4,3,128]{2,1,0:T(4,128)S(1)}, f32[4,3,128,2048]{2,3,1,0}) fusion(pred[4,128,16,128]{1,3,2,0:T(8,128)(4,1)S(1)} %or_and_fusion.2, bf16[4,3,128,2048]{2,3,1,0:T(8,128)(2,1)} %bitcast.172, bf16[1,4,128,3,128]{4,2,3,1,0:T(8,128)(2,1)S(1)} %copy.214), kind=kOutput, calls=%fused_computation.5.clone.1 | convolution fusion | flops 814742016 | bytes 20322304 | tf_op jit(solution)/shard_map/while
  502.0 6.4 gather_fusion.1
  508.4 8.6 %copy.215 = bf16[64,128,384]{1,2,0:T(8,128)(2,1)} copy(bf16[64,128,384]{2,1,0:T(8,128)(2,1)} %gather_fusion.1) | data formatting | bytes 12582912 | tf_op jit(solution)/shard_map/while/body/eval_jaxpr/gather | solution.py:135
  517.0 7.7 %fusion.82 = f32[4,3,128]{2,1,0:T(4,128)S(1)} fusion(f32[4,3,128,2048]{2,3,1,0} %get-tuple-element.466, f32[4,3,128]{2,1,0:T(4,128)S(1)} %get-tuple-element.467, pred[4,128,16,128]{1,3,2,0:T(8,128)(4,1)} %copy-done.1), kind=kLoop, calls=%fused_computation.6.clone.1 | loop fusion | flops 12581376 | bytes 13643776 | tf_op jit(solution)/shard_map/while/body/eval_jaxpr/reduce_sum | solution.py:148
  525.4 7.5 %fusion.83 = bf16[1,4,128,3,128]{2,4,3,1,0:T(8,128)(2,1)S(1)} fusion(f32[4,3,128,2048]{2,3,1,0:S(1)} %copy-done, f32[4,3,128]{2,1,0:T(4,128)S(1)} %get-tuple-element.467, pred[4,128,16,128]{1,3,2,0:T(8,128)(4,1)} %copy-done.1, bf16[4,16,128,3,128]{2,4,3,1,0:T(8,128)(2,1)} %bitcast.175, f32[4,128,3]{1,2,0:T(4,128)S(1)} %bitcast.192), kind=kOutput, calls=%fused_computation.18.clone.1 | convolution fusion | flops 818282496 | bytes 20328448 | tf_op jit(solution)/shard_map/while/body/eval_jaxpr/ghtjs,gjshe->gthe/dot_general | solution.py:149
  535.7 6.7 %gather_fusion = bf16[64,128,384]{2,1,0:T(8,128)(2,1)} fusion(bf16[48,128,384]{2,1,0:T(8,128)(2,1)} %get-tuple-element.545, s32[1024]{0:T(1024)S(1)} %pad_clamp_fusion.2), kind=kCustom, calls=%fused_computation.1.clone.clone.1 | custom fusion | bytes 12583168 | tf_op jit(solution)/shard_map/while/body/eval_jaxpr/gather | solution.py:134
  542.3 8.6 %copy.212 = bf16[64,128,384]{1,2,0:T(8,128)(2,1)} copy(bf16[64,128,384]{2,1,0:T(8,128)(2,1)} %gather_fusion) | data formatting | bytes 12582912 | tf_op jit(solution)/shard_map/while/body/eval_jaxpr/gather | solution.py:134
  551.0 8.6 %copy.213 = bf16[4,16,128,3,128]{4,2,1,3,0:T(8,128)(2,1)} copy(bf16[4,16,128,3,128]{2,4,3,1,0:T(8,128)(2,1)} %bitcast.171) | data formatting | bytes 12582912 | tf_op jit(solution)/shard_map/while/body/eval_jaxpr/reshape | solution.py:134
  561.0 9.4 %fusion.81 = (f32[4,3,128]{2,1,0:T(4,128)S(1)}, f32[4,3,128,2048]{2,3,1,0}) fusion(pred[4,128,16,128]{1,3,2,0:T(8,128)(4,1)S(1)} %or_and_fusion.2, bf16[4,3,128,2048]{2,3,1,0:T(8,128)(2,1)} %bitcast.172, bf16[1,4,128,3,128]{4,2,3,1,0:T(8,128)(2,1)S(1)} %copy.214), kind=kOutput, calls=%fused_computation.5.clone.1 | convolution fusion | flops 814742016 | bytes 20322304 | tf_op jit(solution)/shard_map/while
  570.4 6.4 gather_fusion.1
  576.8 8.6 %copy.215 = bf16[64,128,384]{1,2,0:T(8,128)(2,1)} copy(bf16[64,128,384]{2,1,0:T(8,128)(2,1)} %gather_fusion.1) | data formatting | bytes 12582912 | tf_op jit(solution)/shard_map/while/body/eval_jaxpr/gather | solution.py:135
  585.4 7.7 %fusion.82 = f32[4,3,128]{2,1,0:T(4,128)S(1)} fusion(f32[4,3,128,2048]{2,3,1,0} %get-tuple-element.466, f32[4,3,128]{2,1,0:T(4,128)S(1)} %get-tuple-element.467, pred[4,128,16,128]{1,3,2,0:T(8,128)(4,1)} %copy-done.1), kind=kLoop, calls=%fused_computation.6.clone.1 | loop fusion | flops 12581376 | bytes 13643776 | tf_op jit(solution)/shard_map/while/body/eval_jaxpr/reduce_sum | solution.py:148
  593.8 7.5 %fusion.83 = bf16[1,4,128,3,128]{2,4,3,1,0:T(8,128)(2,1)S(1)} fusion(f32[4,3,128,2048]{2,3,1,0:S(1)} %copy-done, f32[4,3,128]{2,1,0:T(4,128)S(1)} %get-tuple-element.467, pred[4,128,16,128]{1,3,2,0:T(8,128)(4,1)} %copy-done.1, bf16[4,16,128,3,128]{2,4,3,1,0:T(8,128)(2,1)} %bitcast.175, f32[4,128,3]{1,2,0:T(4,128)S(1)} %bitcast.192), kind=kOutput, calls=%fused_computation.18.clone.1 | convolution fusion | flops 818282496 | bytes 20328448 | tf_op jit(solution)/shard_map/while/body/eval_jaxpr/ghtjs,gjshe->gthe/dot_general | solution.py:149
  602.4 2.8 all_to_all.47
  606.7 4.2 all-to-all-start.2
  612.5 20.0 %all-to-all-done.2 = bf16[8,256,384]{1,2,0:T(8,128)(2,1)S(1)} async-done(((bf16[8,256,384]{1,2,0:T(8,128)(2,1)}), bf16[8,256,384]{1,2,0:T(8,128)(2,1)S(1)}, u32[]{:S(2)}, u32[]{:S(2)}) %all-to-all-start.2) | async-done | bytes 1572896 | tf_op jit(solution)/shard_map/all_to_all | solution.py:164
  632.5 1.7 copy.154
  (222 shorter events, 97.0 us)
Async XLA Ops:
  7.2 152.8 %all-gather.4.cloned.1.call-start = ((), (), s32[]{:S(2)}) async-start(), calls=%async_computation.3 | async-start | bytes 6488064 | tf_op jit(solution)/shard_map/all_gather | solution.py:17
  12.1 1.6 copy-start.6
  21.1 2.6 copy-start.5
  55.6 0.7 copy-start.2
  58.9 7.1 %copy-start.10 = (u32[256]{0:T(256)S(1)}, u32[256]{0:T(256)}, u32[]{:S(2)}) copy-start(u32[256]{0:T(256)} %constant.97) | copy-start | bytes 3076
  61.5 72.4 %all-to-all-start.1 = ((bf16[256,8,384]{2,0,1:T(8,128)(2,1)}), bf16[256,8,384]{2,0,1:T(8,128)(2,1)}, u32[]{:S(2)}, u32[]{:S(2)}) async-start(bf16[256,8,384]{2,0,1:T(8,128)(2,1)} %copy.148), calls=%async_computation.1 | async-start | bytes 3145728 | tf_op jit(solution)/shard_map/all_to_all | solution.py:103
  133.9 79.5 %collective-permute-start.2 = (bf16[2048,384]{1,0:T(8,128)(2,1)}, bf16[2048,384]{1,0:T(8,128)(2,1)}, u32[]{:S(2)}, u32[]{:S(2)}) collective-permute-start(bf16[2048,384]{1,0:T(8,128)(2,1)} %bitcast.19), channel_id=1, source_target_pairs={{0,8},{8,16},{16,24},{24,32},{32,40},{40,48},{48,56},{56,64},{64,7... | collective-permute-start | bytes 4718600 | tf_op jit(solution)/shard_map/ppermute | solution.py:35
  203.2 5.6 copy-start.9
  209.3 7.3 %copy-start.7 = (bf16[256,3072]{1,0:T(8,128)(2,1)S(1)}, bf16[256,3072]{1,0:T(8,128)(2,1)}, u32[]{:S(2)}) copy-start(bf16[256,3072]{1,0:T(8,128)(2,1)} %param.19) | copy-start | bytes 4718596
  210.8 107.6 %copy-start.3 = (bf16[48,8,16,128]{3,1,2,0:T(8,128)(2,1)}, bf16[48,8,16,128]{3,1,2,0:T(8,128)(2,1)S(1)}, u32[]{:S(2)}) copy-start(bf16[48,8,16,128]{3,1,2,0:T(8,128)(2,1)S(1)} %copy.202) | copy-start | bytes 4718596
  210.8 44.2 %copy-start.8 = (s32[16,16]{1,0:T(8,128)S(1)}, s32[16,16]{1,0:T(8,128)}, u32[]{:S(2)}) copy-start(s32[16,16]{1,0:T(8,128)} %param.21) | copy-start | bytes 3076
  210.8 42.2 %collective-permute-start = (bf16[2048,384]{0,1:T(8,128)(2,1)S(1)}, bf16[2048,384]{0,1:T(8,128)(2,1)}, u32[]{:S(2)}, u32[]{:S(2)}) collective-permute-start(bf16[2048,384]{0,1:T(8,128)(2,1)S(1)} %bitcast.176), channel_id=1, source_target_pairs={{0,8},{8,16},{16,24},{24,32},{32,40},{40,48},{48,56},{56,64},{64,7... | collective-permute-start | bytes 4718600 | tf_op jit(solution)/shard_map/ppermute | solution.py:35
  213.4 73.4 %collective-permute-start.3 = (bf16[2048,384]{1,0:T(8,128)(2,1)}, bf16[2048,384]{1,0:T(8,128)(2,1)}, u32[]{:S(2)}, u32[]{:S(2)}) collective-permute-start(bf16[2048,384]{1,0:T(8,128)(2,1)} %collective-permute-done.2), channel_id=1, source_target_pairs={{0,8},{8,16},{16,24},{24,32},{32,40},{40,48},{48,56},{56,64},{64,7... | collective-permute-start | bytes 4718600 | tf_op jit(solution)/shard_map/ppermute | solution.py:35
  218.2 37.3 %all-to-all-start = ((bf16[256,8,384]{0,2,1:T(8,128)(2,1)}), bf16[256,8,384]{0,2,1:T(8,128)(2,1)S(1)}, u32[]{:S(2)}, u32[]{:S(2)}) async-start(bf16[256,8,384]{0,2,1:T(8,128)(2,1)} %bitcast.184), calls=%async_computation | async-start | bytes 3145728 | tf_op jit(solution)/shard_map/all_to_all | solution.py:102
  253.1 65.3 %collective-permute-start.1 = (bf16[2048,384]{0,1:T(8,128)(2,1)}, bf16[2048,384]{0,1:T(8,128)(2,1)}, u32[]{:S(2)}, u32[]{:S(2)}) collective-permute-start(bf16[2048,384]{0,1:T(8,128)(2,1)} %collective-permute-done), channel_id=1, source_target_pairs={{0,8},{8,16},{16,24},{24,32},{32,40},{40,48},{48,56},{56,64},{64,7... | collective-permute-start | bytes 4718600 | tf_op jit(solution)/shard_map/ppermute | solution.py:35
  330.3 25.5 %copy-start.1 = (pred[4,128,16,128]{1,3,2,0:T(8,128)(4,1)}, pred[4,128,16,128]{1,3,2,0:T(8,128)(4,1)S(1)}, u32[]{:S(2)}) copy-start(pred[4,128,16,128]{1,3,2,0:T(8,128)(4,1)S(1)} %or_and_fusion.2) | copy-start | bytes 3145732 | tf_op jit(solution)/shard_map/while
  380.1 8.5 %copy-start = (f32[4,3,128,2048]{2,3,1,0:S(1)}, f32[4,3,128,2048]{2,3,1,0}, u32[]{:S(2)}) copy-start(f32[4,3,128,2048]{2,3,1,0} %get-tuple-element.466) | copy-start | bytes 37748740 | tf_op jit(solution)/shard_map/while
  398.7 25.5 %copy-start.1 = (pred[4,128,16,128]{1,3,2,0:T(8,128)(4,1)}, pred[4,128,16,128]{1,3,2,0:T(8,128)(4,1)S(1)}, u32[]{:S(2)}) copy-start(pred[4,128,16,128]{1,3,2,0:T(8,128)(4,1)S(1)} %or_and_fusion.2) | copy-start | bytes 3145732 | tf_op jit(solution)/shard_map/while
  448.6 8.5 %copy-start = (f32[4,3,128,2048]{2,3,1,0:S(1)}, f32[4,3,128,2048]{2,3,1,0}, u32[]{:S(2)}) copy-start(f32[4,3,128,2048]{2,3,1,0} %get-tuple-element.466) | copy-start | bytes 37748740 | tf_op jit(solution)/shard_map/while
  467.1 25.5 %copy-start.1 = (pred[4,128,16,128]{1,3,2,0:T(8,128)(4,1)}, pred[4,128,16,128]{1,3,2,0:T(8,128)(4,1)S(1)}, u32[]{:S(2)}) copy-start(pred[4,128,16,128]{1,3,2,0:T(8,128)(4,1)S(1)} %or_and_fusion.2) | copy-start | bytes 3145732 | tf_op jit(solution)/shard_map/while
  517.0 8.5 %copy-start = (f32[4,3,128,2048]{2,3,1,0:S(1)}, f32[4,3,128,2048]{2,3,1,0}, u32[]{:S(2)}) copy-start(f32[4,3,128,2048]{2,3,1,0} %get-tuple-element.466) | copy-start | bytes 37748740 | tf_op jit(solution)/shard_map/while
  535.6 25.5 %copy-start.1 = (pred[4,128,16,128]{1,3,2,0:T(8,128)(4,1)}, pred[4,128,16,128]{1,3,2,0:T(8,128)(4,1)S(1)}, u32[]{:S(2)}) copy-start(pred[4,128,16,128]{1,3,2,0:T(8,128)(4,1)S(1)} %or_and_fusion.2) | copy-start | bytes 3145732 | tf_op jit(solution)/shard_map/while
  585.4 8.5 %copy-start = (f32[4,3,128,2048]{2,3,1,0:S(1)}, f32[4,3,128,2048]{2,3,1,0}, u32[]{:S(2)}) copy-start(f32[4,3,128,2048]{2,3,1,0} %get-tuple-element.466) | copy-start | bytes 37748740 | tf_op jit(solution)/shard_map/while
  605.2 5.7 copy-start.4
  606.7 25.8 %all-to-all-start.2 = ((bf16[8,256,384]{1,2,0:T(8,128)(2,1)}), bf16[8,256,384]{1,2,0:T(8,128)(2,1)S(1)}, u32[]{:S(2)}, u32[]{:S(2)}) async-start(bf16[8,256,384]{1,2,0:T(8,128)(2,1)} %copy.152), calls=%async_computation.2 | async-start | bytes 3145728 | tf_op jit(solution)/shard_map/all_to_all | solution.py:164
Sparse Core Ops, SparseCore 0:
  56.4 103.4 all-gather.3
where the time goes:
time: 646 us; the launch traced here: 641 us
  local copies, waits for them, and re-layouts  208 us (32%)
  waiting for transfers between devices  126 us (20%)
  other arithmetic  114 us (18%)
  matrix products  86.4 us (13%)
  blocking collectives  66.3 us (10%)
  starting transfers between devices  23.3 us (4%)
  between operations  15 us (2%)
    ppermute x4, waiting for transfers between devices, passed_along(): return lax.ppermute(array, axis, pairs)  81.9 us
    unnamed x1, blocking collectives  66.3 us
    gather x8, local copies, waits for them, and re-layouts, attend(): near_keys[slot_index].reshape(group_size, NB, BLK, head_count, HD)  61.1 us
    gather x8, local copies, waits for them, and re-layouts, attend(): near_values[slot_index].reshape(group_size, NB, BLK, head_count, HD)  59.9 us
    while x4, matrix products  37.6 us
    reshape x4, local copies, waits for them, and re-layouts, attend(): near_keys[slot_index].reshape(group_size, NB, BLK, head_count, HD)  34.5 us
    select_n x32, other arithmetic, turn(): return jax.tree.map(lambda a, b: jnp.where(reached, a, b), new, before)  32.7 us
    reduce_sum x4, other arithmetic, attend(): row_total = jnp.sum(weights, axis=(3, 4))  30.7 us
  transfers between devices with their start and end apart: 8, of which 5 were waited for; matrix products, arithmetic and copies ran while one was open for 11% of the time, Pallas kernels for 0%

commit v1 on v0

v1 whole, which is shorter than its diff:
```python
import functools
import math

import jax
import jax.numpy as jnp
from jax import lax
from jax.experimental import pallas as pl
from jax.experimental.pallas import tpu as pltpu
from jax.sharding import PartitionSpec as P

HD = 128
BLK = 128
NB = 16
EPSILON = 1e-06
MESH = pl.DeviceIdType.MESH
F32 = jnp.float32
BF16 = jnp.bfloat16
SCALE = HD ** (-0.5) * math.log2(math.e)
HIDDEN = -1e30
FLOOR = -1e20

NH = 3
HEADS = 8
ZS, YS = 8, 4
NCTX = ZS * YS
TOK = 2048
NBL = TOK // BLK
SUB = TOK // HEADS
WIDTH = NH * HD
PIECE = WIDTH // ZS
CHUNK = 512
PAIR = 2 * BLK
NPAIR = TOK // PAIR


def dot(a, b, ca=1, cb=0):
    return lax.dot_general(a, b, (((ca,), (cb,)), ((), ())), preferred_element_type=F32)


def silu(x):
    v = x.astype(F32)
    return (v / (1.0 + jnp.exp(-v))).astype(BF16)


def body(
    lq_any, lk_any, lv_any, cum_ref, gain_ref, sq_any, sk_any, bias_ref,
    lin_any, soft_any,
    lq, lk, lv, kb, upd, state, lin, vt,
    q0, q1, q2, kk, b1, b2,
    o2s, o1s, o2r, o1r, s2s, s1s, s2r, s1r, ost,
    e1s, e1r, e2r, e2s, e3s, inc,
    load_sem, own_sem, qs_sem, qr_sem, ks_sem, kr_sem, hop_s, hop_r, bias_s, bias_r,
    res_s, res_r, e1_s, e1_r, e2_s, e2_r, e3_s, e3_r, out_s, out_r, fin_sem,
):
    ctx = lax.axis_index("ctx")
    head = lax.axis_index("head")
    y, z = ctx // ZS, ctx % ZS
    prev = (ctx + NCTX - 1) % NCTX
    nxt = (ctx + 1) % NCTX

    def remote(src, dst, ss, rs, c, h):
        return pltpu.make_async_remote_copy(
            src_ref=src, dst_ref=dst, send_sem=ss, recv_sem=rs, device_id=(c, h), device_id_type=MESH
        )

    loads = [
        pltpu.make_async_copy(lk_any, lk, load_sem.at[0]),
        pltpu.make_async_copy(lv_any, lv, load_sem.at[1]),
        pltpu.make_async_copy(lq_any, lq, load_sem.at[2]),
    ]
    for c in loads:
        c.start()

    barrier = pltpu.get_barrier_semaphore()
    greeted = 0
    for o in range(1, HEADS):
        pl.semaphore_signal(barrier, inc=1, device_id=(ctx, (head + o) % HEADS), device_id_type=MESH)
        greeted += 1
    for o in range(1, ZS):
        pl.semaphore_signal(barrier, inc=1, device_id=(y * ZS + (z + o) % ZS, head), device_id_type=MESH)
        greeted += 1
    for o in range(1, YS):
        pl.semaphore_signal(barrier, inc=1, device_id=(((y + o) % YS) * ZS + z, head), device_id_type=MESH)
        greeted += 1
    for c in (prev, nxt):
        pl.semaphore_signal(barrier, inc=1, device_id=(c, head), device_id_type=MESH)
        greeted += 1
    pl.semaphore_wait(barrier, greeted)

    def regroup(src, dst, h, o, ss, rs):
        peer = (head + o) % HEADS
        col = pl.multiple_of(peer * WIDTH + h * HD, HD)
        row = pl.multiple_of(head * SUB, SUB)
        return remote(src.at[:, pl.ds(col, HD)], dst.at[h, pl.ds(row, SUB), :], ss.at[h, o], rs.at[h, o], ctx, peer)

    def own_part(src, dst, h, sem):
        col = pl.multiple_of(head * WIDTH + h * HD, HD)
        row = pl.multiple_of(head * SUB, SUB)
        return pltpu.make_async_copy(src.at[:, pl.ds(col, HD)], dst.at[h, pl.ds(row, SUB), :], sem)

    order = (1, 7, 2, 6, 3, 5, 4)
    for h in range(NH):
        own_part(sq_any, q0, h, own_sem.at[0, h]).start()
        for o in order:
            regroup(sq_any, q0, h, o, qs_sem, qr_sem).start()
    for h in range(NH):
        own_part(sk_any, kk, h, own_sem.at[1, h]).start()
        for o in order:
            regroup(sk_any, kk, h, o, ks_sem, kr_sem).start()

    bias_hop1 = remote(bias_ref.at[pl.ds(1, 2)], b1, bias_s.at[0], bias_r.at[0], prev, head)
    bias_hop2 = remote(b1.at[1], b2, bias_s.at[1], bias_r.at[1], prev, head)

    def hop1(h):
        return remote(q0.at[h], q1.at[h], hop_s.at[0, h], hop_r.at[0, h], prev, head)

    def hop2(h):
        return remote(q1.at[h], q2.at[h], hop_s.at[1, h], hop_r.at[1, h], prev, head)

    def start_hop1(h):
        own_part(sq_any, q0, h, own_sem.at[0, h]).wait()
        for o in order:
            regroup(sq_any, q0, h, o, qs_sem, qr_sem).wait_recv()
        hop1(h).start()

    def start_hop2(h):
        hop1(h).wait_recv()
        hop2(h).start()

    loads[0].wait()
    loads[1].wait()
    state[...] = jnp.zeros_like(state)

    def block_decay(h, n):
        row = cum_ref[h, pl.ds(n, 1), :]
        rowb = jnp.broadcast_to(row, (BLK, BLK))
        return row[:, BLK - 1 :], rowb, rowb.T

    def gather_state(n, carry):
        at = pl.multiple_of(n * BLK, BLK)
        for h in range(NH):
            total, _, colb = block_decay(h, n)
            key = silu(lk[pl.ds(at, BLK), h * HD : (h + 1) * HD])
            kb[h, pl.ds(at, BLK), :] = key
            value = lv[pl.ds(at, BLK), h * HD : (h + 1) * HD]
            weighted = key.astype(F32) * jnp.exp(total - colb)
            high = weighted.astype(BF16)
            low = (weighted - high.astype(F32)).astype(BF16)
            update = dot(high, value, 0, 0) + dot(low, value, 0, 0)
            upd[h, n] = update
            rows = slice(h * HD, (h + 1) * HD)
            state[rows, :] = jnp.exp(total) * state[rows, :] + update
        return carry

    lax.fori_loop(0, NBL // 2, gather_state, 0)
    start_hop1(0)
    bias_hop1.start()
    lax.fori_loop(NBL // 2, NBL, gather_state, 0)

    for h in range(NH):
        total = jnp.sum(cum_ref[h], axis=0, keepdims=True)[:, BLK - 1 :]
        e1s[:, PIECE + h, :] = jnp.broadcast_to(jnp.exp(total), (ZS, HD))
    for p in range(ZS):
        e1s[p, :PIECE, :] = state[p * PIECE : (p + 1) * PIECE, :]

    def e1_copy(o):
        peer = (z + o) % ZS
        return remote(e1s.at[peer], e1r.at[z], e1_s.at[o], e1_r.at[o], y * ZS + peer, head)

    def e2_copy(o):
        peer = (y + o) % YS
        return remote(e2s, e2r.at[y], e2_s.at[o], e2_r.at[o], peer * ZS + z, head)

    def e3_copy(o):
        peer = (z + o) % ZS
        rows = pl.ds(pl.multiple_of(z * PIECE, PIECE), PIECE)
        return remote(e3s.at[peer], inc.at[rows, :], e3_s.at[o], e3_r.at[o], y * ZS + peer, head)

    for o in range(1, ZS):
        e1_copy(o).start()
    start_hop1(1)
    e1r[z] = e1s[z]
    for o in range(1, ZS):
        e1_copy(o).wait_recv()
    place = z * PIECE + lax.broadcasted_iota(jnp.int32, (PIECE, HD), 0)
    acc = jnp.zeros((PIECE, HD), F32)
    reach = jnp.ones((PIECE, HD), F32)
    reaches = []
    for s in range(ZS):
        e3s[s] = acc
        reaches.append(reach)
        d = [e1r[s, PIECE + h : PIECE + h + 1, :] for h in range(NH)]
        step = jnp.where(place < HD, d[0], jnp.where(place < 2 * HD, d[1], d[2]))
        acc = step * acc + e1r[s, :PIECE, :]
        reach = reach * step
    e2s[:PIECE, :] = acc
    e2s[PIECE:, :] = reach
    for o in range(1, YS):
        e2_copy(o).start()
    start_hop1(2)
    e2r[y] = e2s[...]
    for o in range(1, YS):
        e2_copy(o).wait_recv()
    offset = jnp.zeros((PIECE, HD), F32)
    for s in range(YS):
        new = e2r[s, PIECE:, :] * offset + e2r[s, :PIECE, :]
        offset = jnp.where(s < y, new, offset)
    for s in range(ZS):
        e3s[s] = e3s[s] + reaches[s] * offset
    for o in range(1, ZS):
        e3_copy(o).start()
    inc[pl.ds(pl.multiple_of(z * PIECE, PIECE), PIECE), :] = e3s[z]
    loads[2].wait()
    for o in range(1, ZS):
        e3_copy(o).wait_recv()

    causal = lax.broadcasted_iota(jnp.int32, (BLK, BLK), 0) >= lax.broadcasted_iota(jnp.int32, (BLK, BLK), 1)

    def mix(h):
        gain = gain_ref[h : h + 1, :]

        def two(g, kv):
            for u in range(2):
                n = 2 * g + u
                at = pl.multiple_of(n * BLK, BLK)
                total, rowb, colb = block_decay(h, n)
                query = silu(lq[pl.ds(at, BLK), h * HD : (h + 1) * HD])
                key = kb[h, pl.ds(at, BLK), :]
                value = lv[pl.ds(at, BLK), h * HD : (h + 1) * HD]
                high = kv.astype(BF16)
                low = (kv - high.astype(F32)).astype(BF16)
                inter = jnp.exp(colb) * (dot(query, high) + dot(query, low))
                gap = jnp.where(causal, colb - rowb, HIDDEN)
                weights = (dot(query, key, 1, 1) * jnp.exp(gap)).astype(BF16)
                mixed = dot(weights, value) + inter
                square = jnp.mean(mixed * mixed, axis=-1, keepdims=True)
                normed = mixed * lax.rsqrt(square + EPSILON) * gain
                lin[h, pl.ds(at, BLK), :] = normed.astype(BF16)
                vt[h, :, pl.ds(at, BLK)] = normed.T.astype(BF16)
                kv = jnp.exp(total) * kv + upd[h, n]
            return kv

        lax.fori_loop(0, NBL // 2, two, inc[h * HD : (h + 1) * HD, :])
        store_lin(h).start()

    def store_lin(h):
        return pltpu.make_async_copy(lin.at[h], lin_any.at[:, pl.ds(h * HD, HD)], fin_sem.at[h])

    mix(0)
    start_hop2(0)
    bias_hop1.wait_recv()
    bias_hop2.start()
    mix(1)
    start_hop2(1)
    mix(2)

    key_row = lax.broadcasted_iota(jnp.int32, (CHUNK, PAIR), 0)
    query_lane = lax.broadcasted_iota(jnp.int32, (CHUNK, PAIR), 1)
    per = CHUNK // BLK

    def attend(h, queries, bias, role, finish):
        def pair_body(p, carry):
            lanes = pl.ds(pl.multiple_of(p * PAIR, PAIR), PAIR)
            query = queries[lanes, :]

            def step(c, state3, diagonal=False):
                m, l, acc = state3
                at = c * CHUNK if isinstance(c, int) else pl.multiple_of(c * CHUNK, CHUNK)
                logits = dot(kk[h, pl.ds(at, CHUNK), :], query, 1, 1)
                if diagonal:
                    logits = jnp.where(key_row + c * CHUNK <= query_lane + p * PAIR, logits, HIDDEN)
                parts = [logits[j * BLK : (j + 1) * BLK, :] for j in range(per)]
                pens = [bias[pl.ds(c * per + j, 1), lanes] for j in range(per)]
                new = m
                for part, pen in zip(parts, pens):
                    new = jnp.maximum(new, jnp.max(part, axis=0, keepdims=True) * SCALE + pen)
                keep = jnp.exp2(m - new)
                l = l * keep
                weights = []
                for part, pen in zip(parts, pens):
                    w = jnp.exp2(part * SCALE + (pen - new))
                    l = l + jnp.sum(w, axis=0, keepdims=True)
                    weights.append(w.astype(BF16))
                acc = acc * keep + dot(vt[h, :, pl.ds(at, CHUNK)], jnp.concatenate(weights, axis=0))
                return new, l, acc

            start = (
                jnp.full((1, PAIR), FLOOR, F32),
                jnp.zeros((1, PAIR), F32),
                jnp.zeros((HD, PAIR), F32),
            )
            if role == 1:
                result = start
                for c in range(TOK // CHUNK):
                    result = step(c, result)
            elif role == 2:
                result = lax.fori_loop(p // 2, TOK // CHUNK, step, start)
            else:
                result = lax.fori_loop(0, p // 2, step, start)
                result = step(p // 2, result, diagonal=True)
            finish(p, lanes, result)
            return carry

        lax.fori_loop(0, NPAIR, pair_body, 0)

    def merged(h, p, lanes, result, part, stats):
        m, l, acc = result
        m_in = stats[h, pl.ds(p, 1), :]
        l_in = stats[h, pl.ds(NPAIR + p, 1), :]
        new = jnp.maximum(m, m_in)
        mine, theirs = jnp.exp2(m - new), jnp.exp2(m_in - new)
        return new, l * mine + l_in * theirs, acc * mine + part[h, :, lanes].astype(F32) * theirs

    def store_part(h, p, lanes, result, part, stats):
        m, l, acc = result
        part[h, :, lanes] = acc.astype(BF16)
        stats[h, pl.ds(p, 1), :] = m
        stats[h, pl.ds(NPAIR + p, 1), :] = l

    def forward(h, role):
        o_s, o_r, s_s, s_r = (o2s, o2r, s2s, s2r) if role == 2 else (o1s, o1r, s1s, s1r)
        return (
            remote(o_s.at[h], o_r.at[h], res_s.at[role, 0, h], res_r.at[role, 0, h], nxt, head),
            remote(s_s.at[h], s_r.at[h], res_s.at[role, 1, h], res_r.at[role, 1, h], nxt, head),
        )

    def out_copy(h, o):
        peer = (head + o) % HEADS
        rows = pl.ds(pl.multiple_of(peer * SUB, SUB), SUB)
        col = pl.ds(pl.multiple_of(head * WIDTH + h * HD, HD), HD)
        return remote(ost.at[h, rows, :], soft_any.at[:, col], out_s.at[h, o], out_r.at[h, o], ctx, peer)

    def out_own(h):
        rows = pl.ds(pl.multiple_of(head * SUB, SUB), SUB)
        col = pl.ds(pl.multiple_of(head * WIDTH + h * HD, HD), HD)
        return pltpu.make_async_copy(ost.at[h, rows, :], soft_any.at[:, col], fin_sem.at[NH + h])

    def role2(h):
        hop2(h).wait_recv()
        attend(h, q2.at[h], b2, 2, lambda p, lanes, r: store_part(h, p, lanes, r, o2s, s2s))
        for c in forward(h, 2):
            c.start()

    def role1(h):
        for c in forward(h, 2):
            c.wait_recv()
        attend(
            h, q1.at[h], b1.at[0], 1,
            lambda p, lanes, r: store_part(h, p, lanes, merged(h, p, lanes, r, o2r, s2r), o1s, s1s),
        )
        for c in forward(h, 1):
            c.start()

    def role0(h):
        for c in forward(h, 1):
            c.wait_recv()

        def finish(p, lanes, r):
            m, l, acc = merged(h, p, lanes, r, o1r, s1r)
            ost[h, lanes, :] = (acc / l).T.astype(BF16)

        attend(h, q0.at[h], bias_ref.at[0], 0, finish)
        out_own(h).start()
        for o in order:
            out_copy(h, o).start()

    def keys_here(h):
        own_part(sk_any, kk, h, own_sem.at[1, h]).wait()
        for o in order:
            regroup(sk_any, kk, h, o, ks_sem, kr_sem).wait_recv()

    bias_hop2.wait_recv()
    keys_here(0)
    role2(0)
    start_hop2(2)
    keys_here(1)
    role2(1)
    role1(0)
    keys_here(2)
    role2(2)
    role1(1)
    role1(2)
    role0(0)
    role0(1)
    role0(2)

    for h in range(NH):
        store_lin(h).wait()
        out_own(h).wait()
        hop1(h).wait_send()
        hop2(h).wait_send()
        for role in (1, 2):
            for c in forward(h, role):
                c.wait_send()
        for o in order:
            regroup(sq_any, q0, h, o, qs_sem, qr_sem).wait_send()
            regroup(sk_any, kk, h, o, ks_sem, kr_sem).wait_send()
            out_copy(h, o).wait()
    bias_hop1.wait_send()
    bias_hop2.wait_send()
    for o in range(1, ZS):
        e1_copy(o).wait_send()
        e3_copy(o).wait_send()
    for o in range(1, YS):
        e2_copy(o).wait_send()


def shards(lin_query, lin_key, lin_value, log_decay, norm_gain, soft_query, soft_key, block_list):
    ctx = lax.axis_index("ctx")
    cumulated = jnp.cumsum(log_decay.reshape(NH, NBL, BLK), axis=2)
    ids = (ctx - jnp.arange(3, dtype=jnp.int32))[:, None] * NBL + jnp.arange(NBL, dtype=jnp.int32)[None, :]
    listed = jnp.any(block_list[None, None, :, :] == ids[:, :, None, None], axis=3) & (ids >= 0)[:, :, None]
    bias = jnp.repeat(jnp.where(listed, 0.0, HIDDEN).astype(F32), BLK, axis=2)
    anywhere = pl.BlockSpec(memory_space=pl.ANY)
    vmem = pl.BlockSpec(memory_space=pltpu.VMEM)
    dma = pltpu.SemaphoreType.DMA
    part = (NH, HD, TOK)
    rows = (NH, TOK, HD)
    stats = (NH, 2 * NPAIR, PAIR)
    return pl.pallas_call(
        body,
        out_shape=(
            jax.ShapeDtypeStruct((TOK, WIDTH), BF16),
            jax.ShapeDtypeStruct((SUB, HEADS * WIDTH), BF16),
        ),
        in_specs=[anywhere, anywhere, anywhere, vmem, vmem, anywhere, anywhere, vmem],
        out_specs=(anywhere, anywhere),
        scratch_shapes=[
            pltpu.VMEM((TOK, WIDTH), BF16),
            pltpu.VMEM((TOK, WIDTH), BF16),
            pltpu.VMEM((TOK, WIDTH), BF16),
            pltpu.VMEM(rows, BF16),
            pltpu.VMEM((NH, NBL, HD, HD), F32),
            pltpu.VMEM((WIDTH, HD), F32),
            pltpu.VMEM(rows, BF16),
            pltpu.VMEM(part, BF16),
            pltpu.VMEM(rows, BF16),
            pltpu.VMEM(rows, BF16),
            pltpu.VMEM(rows, BF16),
            pltpu.VMEM(rows, BF16),
            pltpu.VMEM((2, NBL, TOK), F32),
            pltpu.VMEM((NBL, TOK), F32),
            pltpu.VMEM(part, BF16),
            pltpu.VMEM(part, BF16),
            pltpu.VMEM(part, BF16),
            pltpu.VMEM(part, BF16),
            pltpu.VMEM(stats, F32),
            pltpu.VMEM(stats, F32),
            pltpu.VMEM(stats, F32),
            pltpu.VMEM(stats, F32),
            pltpu.VMEM(rows, BF16),
            pltpu.VMEM((ZS, PIECE + 8, HD), F32),
            pltpu.VMEM((ZS, PIECE + 8, HD), F32),
            pltpu.VMEM((YS, 2 * PIECE, HD), F32),
            pltpu.VMEM((2 * PIECE, HD), F32),
            pltpu.VMEM((ZS, PIECE, HD), F32),
            pltpu.VMEM((WIDTH, HD), F32),
            dma((3,)),
            dma((2, NH)),
            dma((NH, HEADS)),
            dma((NH, HEADS)),
            dma((NH, HEADS)),
            dma((NH, HEADS)),
            dma((2, NH)),
            dma((2, NH)),
            dma((2,)),
            dma((2,)),
            dma((3, 2, NH)),
            dma((3, 2, NH)),
            dma((ZS,)),
            dma((ZS,)),
            dma((YS,)),
            dma((YS,)),
            dma((ZS,)),
            dma((ZS,)),
            dma((NH, HEADS)),
            dma((NH, HEADS)),
            dma((2 * NH,)),
        ],
        compiler_params=pltpu.CompilerParams(
            collective_id=0, has_side_effects=True, vmem_limit_bytes=56 * 1024 * 1024
        ),
        cost_estimate=pl.CostEstimate(flops=20_000_000_000, bytes_accessed=12_000_000, transcendentals=30_000_000),
    )(
        lin_query, lin_key, lin_value, cumulated, norm_gain.reshape(NH, HD), soft_query, soft_key, bias
    )


def solution(mesh):
    placed = (
        P("ctx", "head"),
        P("ctx", "head"),
        P("ctx", "head"),
        P("head", "ctx"),
        P("head"),
        P(("ctx", "head"), None),
        P(("ctx", "head"), None),
        P("ctx", None),
    )
    return jax.shard_map(
        shards,
        mesh=mesh,
        in_specs=placed,
        out_specs=(P("ctx", "head"), P(("ctx", "head"), None)),
        check_vma=False,
    )
```

time: 646 us -> 224 us (0.35)
  Pallas kernels: 0 us -> 212 us
  local copies, waits for them, and re-layouts: 208 us -> 5.71 us
  waiting for transfers between devices: 126 us -> 0 us
  other arithmetic: 114 us -> 3.65 us
  matrix products: 86.4 us -> 0 us
  blocking collectives: 66.3 us -> 0 us
  starting transfers between devices: 23.3 us -> 0 us
  between operations: 15 us -> 0.67 us
    pallas_call x0 -> x1, Pallas kernels: none -> 212 us  [shards(): pl.pallas_call(body, out_shape=(jax.ShapeDtypeStruct((TOK, WIDTH), BF16),...]
    gather x16 -> x0, local copies, waits for them, and re-layouts: 121 us -> none  [the longest x8 61.1 us: attend(): near_keys[slot_index].reshape(group_size, NB, BLK, head_count, HD)]
    ppermute x4 -> x0, waiting for transfers between devices: 81.9 us -> none  [passed_along(): return lax.ppermute(array, axis, pairs)]
    unnamed x1 -> x0, blocking collectives: 66.3 us -> none
    dot_general x7 -> x0, matrix products: 48.8 us -> none  [the longest x4 30.1 us: attend(): jnp.einsum('ghtjs,gjshe->gthe', weights.astype(jnp.bfloat16), value_block...]
    while x4 -> x0, matrix products: 37.6 us -> none
    reshape x5 -> x1, local copies, waits for them, and re-layouts: 38 us -> 0.81 us  [shards(): bias = jnp.repeat(jnp.where(listed, 0.0, HIDDEN).astype(F32), BLK, axis=2)]
    select_n x37 -> x1, other arithmetic: 32.8 us -> 0.08 us  [shards(): bias = jnp.repeat(jnp.where(listed, 0.0, HIDDEN).astype(F32), BLK, axis=2)]
  transfers between devices with their start and end apart: 8 -> 0, of which waited for: 5 -> 0; matrix products, arithmetic and copies ran while one was open for 11% -> 0% of each run, Pallas kernels for 0% -> 0%
where the time goes in v1:
time: 224 us; the launch traced here: 222 us
  Pallas kernels  212 us (95%)
  local copies, waits for them, and re-layouts  5.71 us (3%)
  other arithmetic  3.65 us (2%)
    pallas_call x1, Pallas kernels, shards(): pl.pallas_call(body, out_shape=(jax.ShapeDtypeStruct((TOK, WIDTH), BF16),...  212 us
    unnamed x5, local copies, waits for them, and re-layouts  4.74 us

profile of v1, /device:TPU:16, one launch (start us, length us, event | category | flops | bytes accessed | tf_op | source)
XLA Modules:
  0.0 222.0 jit_solution(6463634260334210375)
XLA Ops:
  0.6 0.1 broadcast_compare_fusion
  0.7 0.1 iota_add_fusion
  0.8 1.7 compare_reduce_fusion
  2.5 0.1 and_select_fusion
  2.5 0.8 copy.12
  3.3 1.8 reduce_window_sum.11.cum_ref
  5.1 0.2 broadcast_in_dim.18
  5.2 0.8 reshape.63.bias_ref
  6.0 212.0 %shard_map.95 = (bf16[2048,384]{1,0:T(8,128)(2,1)}, bf16[256,3072]{1,0:T(8,128)(2,1)}) custom-call(bf16[2048,384]{1,0:T(8,128)(2,1)} %lq_any.1, bf16[2048,384]{1,0:T(8,128)(2,1)} %lk_any.1, bf16[2048,384]{1,0:T(8,128)(2,1)} %lv_any.1, f32[3,16,128]{2,1,0:T(8,128)} %reduce_window_sum.11.cum_ref, f32[3,128]{1,0:T(4,128)} %bitcast.9, bf16[256,3072]{1,0:T(8,128)(2,1)} %sq_any.1, ...), custom_call_target="tpu_custom_call" | custom-call | flops 20000000000 | bytes 12000000 | tf_op jit(solution)/shard_map/pallas_call | solution.py:420
  218.0 0.0 copy-start
  218.1 2.8 %copy.15 = bf16[2048,384]{1,0:T(8,128)(2,1)} copy(bf16[2048,384]{1,0:T(8,128)(2,1)} %get-tuple-element.4) | data formatting | bytes 3145728
  220.9 0.0 copy-done
  220.9 1.1 copy.16
  (1 shorter events, 0.0 us)
Async XLA Ops:
  218.0 2.8 %copy-start = (bf16[256,3072]{1,0:T(8,128)(2,1)S(1)}, bf16[256,3072]{1,0:T(8,128)(2,1)}, u32[]{:S(2)}) copy-start(bf16[256,3072]{1,0:T(8,128)(2,1)} %get-tuple-element.5) | copy-start | bytes 4718596
